TPU v7x, 32 devices: a whole 2x2x4 slice. The times are simulated.
32 devices in a mesh: batch: 2 (over y), aux: 4 (over z), ao: 4 (over x, core).
Axes of the slice: x: 2, y: 2, z: 4, core: 2. Of those that a mesh axis runs over, the one named last changes fastest.
Arguments:
- pair_ints: bfloat16 [8, 96, 20480], P(('batch', 'ao'), 'aux'), parts along dimension 0, may hold values from -6 to 6
- batch_energy: float32 [8], P(('batch', 'ao')), parts along dimension 0, may hold values from 0.3 to 3
- occ_energy: float32 [96], P('aux'), may hold values from 0.3 to 3
- occ_coef: bfloat16 [6144, 96], P('ao', 'aux'), may hold values from -0.625 to 0.625
- batch_coef: bfloat16 [6144, 8], P('ao', 'batch'), parts along dimension 1, may hold values from -3 to 3
- deriv: bfloat16 [3, 6144, 20480], P(None, 'ao', 'aux'), may hold values from -0.0390625 to 0.0390625
- owner: int32 [6144], P('ao'), may hold values from 0 to 47, never falling along the last dimension, each value on 1 to 384 neighbouring positions
Outputs:
- amp_ao: bfloat16 [12288, 20480], P(('batch', 'ao'), 'aux'), parts along dimension 0
- gradient: float32 [3, 96], P(None, ('batch', 'aux', 'ao')), parts along dimension 1
There are 2 independent parts, one for each index of `batch`. A program takes and returns all parts, laid end to end along the dimension named above; an argument that names none is the same for every part. Nothing has to cross between parts.
Inputs may be any that keep to these rules, and one draw needn't show every extreme that they name: `owner`: never falls along the AO functions; every atom owns 1 to 384 functions, some atom exactly 384.
All inputs are finite; a program needn't handle non-finite values.
Results may differ from a plain program's by a relative error of at most 0.0051.
Values may be sent and summed in bfloat16 or wider, within the bound.
A program may use at most 320 MiB of HBM per device.

v0:
```python
import jax
import jax.numpy as jnp
from jax import lax
from jax.sharding import PartitionSpec as P

ATOM_DEV = 3


def local(pair_ints, batch_energy, occ_energy, occ_coef, batch_coef, deriv, owner):
    scale = 2.0 / (batch_energy[:, None] + occ_energy[None, :])
    formed = (pair_ints.astype(jnp.float32) * scale[:, :, None]).astype(jnp.bfloat16)
    arrived = lax.all_to_all(formed, "aux", split_axis=2, concat_axis=1, tiled=True)
    coef_all = lax.all_gather(occ_coef, "aux", axis=1, tiled=True)
    weights = batch_coef.astype(jnp.float32)
    initial = jnp.zeros((coef_all.shape[0], arrived.shape[2]), jnp.float32)
    gathered = lax.all_gather(arrived, "ao", axis=0, tiled=True)
    running = initial
    for orbit in range(gathered.shape[0]):
        column = lax.dynamic_slice_in_dim(weights, 0 + orbit, 1, 1)
        running = running + column * jnp.dot(
            coef_all, gathered[orbit], preferred_element_type=jnp.float32
        )
    amp_ao = running.astype(jnp.bfloat16)
    per_func = jnp.einsum("xnp,np->xn", deriv, amp_ao, preferred_element_type=jnp.float32)
    atom_count = ATOM_DEV * lax.axis_size("aux") * lax.axis_size("ao")
    onehot = (owner[:, None] == jnp.arange(atom_count, dtype=jnp.int32)[None, :]).astype(
        jnp.float32
    )
    partial_grad = jnp.dot(per_func, onehot, precision=lax.Precision.HIGHEST)
    totals = lax.psum(partial_grad, ("aux", "ao"))
    own_width = atom_count // (lax.axis_size("aux") * lax.axis_size("ao"))
    gradient = lax.dynamic_slice_in_dim(
        totals, lax.axis_index(("aux", "ao")) * own_width, own_width, 1
    )
    return (amp_ao, gradient)


def solution(mesh):
    return jax.shard_map(
        local,
        mesh=mesh,
        in_specs=(
            P(("batch", "ao"), "aux", None),
            P(("batch", "ao")),
            P("aux"),
            P("ao", "aux"),
            P("ao", "batch"),
            P(None, "ao", "aux"),
            P("ao"),
        ),
        out_specs=(P(("batch", "ao"), "aux"), P(None, ("batch", "aux", "ao"))),
        check_vma=False,
    )
```

profile of v0, /device:TPU:0, one launch (start us, length us, event | category | flops | bytes accessed | tf_op | source)
XLA Modules:
  0.0 531.8 jit_solution(6848069848220704873)
XLA Ops:
  7.9 0.7 add_divide_fusion
  8.5 1.4 multiply_convert_fusion
  10.0 15.2 %copy.17 = bf16[1,24,20480]{1,0,2:T(2,128)(2,1)} copy(bf16[1,24,20480]{2,1,0:T(8,128)(2,1)S(1)} %multiply_convert_fusion) | data formatting | bytes 1966080 | tf_op jit(solution)/shard_map/convert_element_type | solution.py:11
  25.2 0.5 broadcast.19
  25.7 112.9 %reduce.8 = bf16[20480,24]{1,0:T(8,128)(2,1)} reduce(bf16[20480,1,24]{2,1,0:T(2,128)(2,1)} %bitcast.34, bf16[]{:T(256)} %broadcast.19), dimensions={1}, to_apply=%bitcast.20.reduce_sub_computation | reduce | bytes 1966082
  138.6 8.0 %reshape.20 = bf16[4,2,61440]{2,1,0:T(2,128)(2,1)S(1)} reshape(bf16[20480,24]{1,0:T(8,128)(2,1)} %reduce.8) | data formatting | bytes 1966080
  146.6 30.4 %all_to_all.18 = bf16[4,2,61440]{2,1,0:T(2,128)(2,1)S(1)} all-to-all(bf16[4,2,61440]{2,1,0:T(2,128)(2,1)S(1)} %reshape.20), channel_id=1, replica_groups=mesh['batch'=2,'aux'=4,'ao'=4] {'aux'}, dimensions={0} | all-to-all | bytes 1966080 | tf_op jit(solution)/shard_map/all_to_all | solution.py:12
  177.1 14.8 %reshape.21 = bf16[20480,1,24]{2,1,0:T(2,128)(2,1)} reshape(bf16[4,2,61440]{2,1,0:T(2,128)(2,1)S(1)} %all_to_all.18) | data formatting | bytes 1966080
  191.9 18.3 %copy.18 = bf16[1,24,20480]{2,1,0:T(8,128)(2,1)S(1)} copy(bf16[1,24,20480]{1,0,2:T(2,128)(2,1)} %bitcast.35) | data formatting | bytes 1966080 | tf_op jit(solution)/shard_map/all_to_all | solution.py:12
  210.2 0.7 all_to_all.14
  211.0 1.2 copy.19
  212.3 14.5 %all_gather.7 = bf16[1536,96]{0,1:T(8,128)(2,1)S(1)} all-gather(bf16[1536,24]{0,1:T(8,128)(2,1)S(1)} %copy-done.1), channel_id=1, replica_groups=mesh['batch'=2,'aux'=4,'ao'=4] {'aux'}, dimensions={1}, use_global_device_ids=true | all-gather | bytes 368640 | tf_op jit(solution)/shard_map/all_gather | solution.py:13
  226.8 0.1 slice_reduce_fusion.3
  226.9 17.6 %all-gather.2.cloned.1.call-done = bf16[4,96,5120]{2,1,0:T(8,128)(2,1)} async-done(((bf16[1,96,5120]{2,1,0:T(8,128)(2,1)}), bf16[4,96,5120]{2,1,0:T(8,128)(2,1)}) %all-gather.2.cloned.1.call-update) | async-done | bytes 3932176 | tf_op jit(solution)/shard_map/all_gather | solution.py:16
  244.5 13.9 %fusion.2 = f32[5120,1536]{1,0:T(8,128)} fusion(bf16[1536,96]{0,1:T(8,128)(2,1)S(1)} %all_gather.7, bf16[4,96,5120]{2,1,0:T(8,128)(2,1)} %all-gather.2.cloned.1.call-done), kind=kOutput, calls=%fused_computation.6 | convolution fusion | flops 1509949440 | bytes 32735232 | tf_op jit(solution)/shard_map/dot_general | solution.py:20
  258.4 12.4 %fusion.3 = f32[5120,1536]{1,0:T(8,128)} fusion(bf16[1536,96]{0,1:T(8,128)(2,1)S(1)} %all_gather.7, bf16[4,96,5120]{2,1,0:T(8,128)(2,1)S(1)} %copy-done), kind=kOutput, calls=%fused_computation.8 | convolution fusion | flops 1509949440 | bytes 32735232 | tf_op jit(solution)/shard_map/dot_general | solution.py:20
  270.8 12.5 %fusion.4 = f32[5120,1536]{1,0:T(8,128)} fusion(bf16[1536,96]{0,1:T(8,128)(2,1)S(1)} %all_gather.7, bf16[4,96,5120]{2,1,0:T(8,128)(2,1)S(1)} %copy-done), kind=kOutput, calls=%fused_computation.10 | convolution fusion | flops 1509949440 | bytes 32735232 | tf_op jit(solution)/shard_map/dot_general | solution.py:20
  283.2 36.6 %add_convert_fusion = bf16[5120,1536]{1,0:T(8,128)(2,1)} fusion(f32[5120,1536]{1,0:T(8,128)} %fusion.2, f32[5120,1536]{1,0:T(8,128)} %fusion.3, f32[5120,1536]{1,0:T(8,128)} %fusion.4, bf16[1536,96]{0,1:T(8,128)(2,1)S(1)} %all_gather.7, f32[1536]{0:T(1024)S(1)} %get-tuple-element.13, f32[1536]{0:T(1024)S(1)} %get-tuple-element.14, ...), kind=kOutput, calls=%fused_computation.2 | convolution fusion | flops 1572864000 | bytes 111403008 | tf_op jit(solution)/shard_map/dot_general | solution.py:20
  319.8 62.4 %copy.21 = bf16[1536,5120,1]{1,2,0:T(2,128)(2,1)} copy(bf16[1536,5120,1]{0,1,2:T(8,128)(2,1)} %bitcast.32) | data formatting | bytes 31457280 | tf_op jit(solution)/shard_map/add | solution.py:20
  382.2 87.8 %fusion = f32[1536,1,3]{2,1,0:T(1,128)S(1)} fusion(bf16[1536,5120,1]{1,2,0:T(2,128)(2,1)} %copy.21, bf16[3,1536,5120]{2,1,0:T(8,128)(2,1)} %param.12), kind=kOutput, calls=%fused_computation | convolution fusion | flops 47185920 | bytes 62932992 | tf_op jit(solution)/shard_map/xnp,np->xn/dot_general | solution.py:24
  470.0 1.0 fusion.5
  471.0 32.7 %psum.7 = f32[3,48]{1,0:T(4,128)S(1)} all-reduce(f32[3,48]{1,0:T(4,128)S(1)} %fusion.5), channel_id=1, replica_groups=mesh['batch'=2,'aux'=4,'ao'=4] {'aux','ao'}, use_global_device_ids=true, to_apply=%region_0.0 | all-reduce | flops 144 | bytes 1152 | tf_op jit(solution)/shard_map/psum | solution.py:30
  503.7 20.6 %copy.20 = bf16[1536,5120]{1,0:T(8,128)(2,1)} copy(bf16[1536,5120]{0,1:T(8,128)(2,1)} %bitcast.33) | data formatting | bytes 31457280
  524.3 0.6 constant_dynamic-slice_fusion
  (11 shorter events, 0.1 us)
Async XLA Ops:
  7.2 237.3 %all-gather.2.cloned.1.call-start = ((), (), s32[]{:S(2)}) async-start(), calls=%async_computation.1 | async-start | bytes 4915200 | tf_op jit(solution)/shard_map/all_gather | solution.py:16
  10.0 202.3 %copy-start.2 = (bf16[1536,4]{0,1:T(4,128)(2,1)S(1)}, bf16[1536,4]{0,1:T(4,128)(2,1)}, u32[]{:S(2)}) copy-start(bf16[1536,4]{0,1:T(4,128)(2,1)} %param.11) | copy-start | bytes 36868
  10.0 202.3 %copy-start.1 = (bf16[1536,24]{0,1:T(8,128)(2,1)S(1)}, bf16[1536,24]{0,1:T(8,128)(2,1)}, u32[]{:S(2)}) copy-start(bf16[1536,24]{0,1:T(8,128)(2,1)} %param.10) | copy-start | bytes 221188
  244.5 13.9 %copy-start = (bf16[4,96,5120]{2,1,0:T(8,128)(2,1)S(1)}, bf16[4,96,5120]{2,1,0:T(8,128)(2,1)}, u32[]{:S(2)}) copy-start(bf16[4,96,5120]{2,1,0:T(8,128)(2,1)} %all-gather.2.cloned.1.call-done) | copy-start | bytes 11796484
  382.2 87.8 %copy-start.3 = (s32[1536]{0:T(1024)S(1)}, s32[1536]{0:T(1024)}, u32[]{:S(2)}) copy-start(s32[1536]{0:T(1024)} %param.13) | copy-start | bytes 18436
Sparse Core Ops, SparseCore 0:
  212.4 32.0 all-gather.1
where the time goes:
time: 534 us; the launch traced here: 532 us
  matrix products  164 us (31%)
  local copies, waits for them, and re-layouts  143 us (27%)
  other arithmetic  115 us (22%)
  blocking collectives  77.6 us (15%)
  waiting for transfers between devices  17.6 us (3%)
  between operations  14.8 us (3%)
    unnamed x1, other arithmetic  113 us
    dot_general x1, matrix products, local(): jnp.einsum('xnp,np->xn', deriv, amp_ao, preferred_element_type=jnp.float32)  87.8 us
    dot_general x4, matrix products, local(): jnp.dot(coef_all, gathered[orbit], preferred_element_type=jnp.float32)  75.3 us
    add x1, local copies, waits for them, and re-layouts, local(): running + column * jnp.dot(coef_all, gathered[orbit], preferred_element_t...  62.4 us
    unnamed x12, local copies, waits for them, and re-layouts  43.9 us
    psum x1, blocking collectives, local(): totals = lax.psum(partial_grad, ('aux', 'ao'))  32.7 us
    all_to_all x1, blocking collectives, local(): lax.all_to_all(formed, 'aux', split_axis=2, concat_axis=1, tiled=True)  30.4 us
    all_to_all x3, local copies, waits for them, and re-layouts, local(): lax.all_to_all(formed, 'aux', split_axis=2, concat_axis=1, tiled=True)  20.3 us
  transfers between devices with their start and end apart: 1, of which 1 were waited for; matrix products, arithmetic and copies ran while one was open for 0% of the time, Pallas kernels for 0%

commit v1 on v0

v1 whole, which is shorter than its diff:
```python
import functools

import jax
import jax.numpy as jnp
from jax import lax
from jax.experimental import pallas as pl
from jax.experimental.pallas import tpu as pltpu
from jax.sharding import PartitionSpec as P

ATOM_DEV = 3
MESH = pl.DeviceIdType.MESH
F32 = jnp.float32
BF16 = jnp.bfloat16
CHUNK = 512
ROWS = 256
SLOTS = 3
LEAVE = 8


def eye(rows, columns, dtype):
    row = lax.broadcasted_iota(jnp.int32, (rows, columns), 0)
    column = lax.broadcasted_iota(jnp.int32, (rows, columns), 1)
    return (row == column).astype(F32).astype(dtype)


def across(left, right, **kw):
    return lax.dot_general(
        left, right, (((1,), (1,)), ((), ())), preferred_element_type=F32, **kw
    )


def fused_kernel(
    aux, atoms, pair, batch_energy, occ_energy, occ_coef, batch_coef, deriv, owner,
    amp, grad,
    outgoing, arrived, coef, coef_t, weights, packed, slabs, total,
    z_send, z_recv, w_send, w_recv, x_send, x_recv, c_send, c_recv, f_send, f_recv, d_sem,
):
    occ = pair.shape[1]
    width = pair.shape[2] // aux
    chunks = width // CHUNK
    half = CHUNK // 2
    functions = occ_coef.shape[0]
    me_z, me = lax.axis_index("aux"), lax.axis_index("ao")
    far = lax.rem(me + 2, 4)
    near = me + 1 - 2 * lax.rem(me, 2)
    near_far = lax.rem(near + 2, 4)

    def fetch(step):
        return pltpu.make_async_copy(
            deriv.at[:, :, pl.ds(step * CHUNK, CHUNK)], slabs.at[step % SLOTS], d_sem.at[step % SLOTS]
        )

    for step in range(min(SLOTS, chunks)):
        fetch(step).start()

    barrier = pltpu.get_barrier_semaphore()
    for hop in range(1, aux):
        pl.semaphore_signal(
            barrier, inc=1, device_id={"aux": lax.rem(me_z + hop, aux)}, device_id_type=MESH
        )
    for other in (far, near):
        pl.semaphore_signal(barrier, inc=1, device_id={"ao": other}, device_id_type=MESH)

    turned = across(eye(occ, occ, BF16), occ_coef[...])
    coef[me_z] = jnp.concatenate(
        [turned[:, : functions // 2], turned[:, functions // 2 :]], axis=0
    ).astype(BF16)

    scale_row = 2.0 / (batch_energy[0] + occ_energy[...])
    scale = jnp.sum(eye(occ, occ, F32) * scale_row, axis=1, keepdims=True)

    def form(z, step):
        start = pl.multiple_of(z * width + step * CHUNK, CHUNK)
        block = pair[0, :, pl.ds(start, CHUNK)].astype(F32) * scale
        return jnp.concatenate([block[:, :half], block[:, half:]], axis=0).astype(BF16)

    def z_copy(step, hop, source=None):
        z = me_z if source is None else source
        return pltpu.make_async_remote_copy(
            src_ref=outgoing.at[hop - 1, step],
            dst_ref=arrived.at[step, me, z],
            send_sem=z_send.at[step, hop - 1],
            recv_sem=z_recv.at[step, hop - 1],
            device_id={"aux": lax.rem(me_z + hop, aux)},
            device_id_type=MESH,
        )

    def w_copy(hop, source=None):
        z = me_z if source is None else source
        return pltpu.make_async_remote_copy(
            src_ref=coef.at[me_z],
            dst_ref=coef.at[z],
            send_sem=w_send.at[hop - 1],
            recv_sem=w_recv.at[hop - 1],
            device_id={"aux": lax.rem(me_z + hop, aux)},
            device_id_type=MESH,
        )

    def slot_copy(step, slot, sends, recvs, target, source=None):
        return pltpu.make_async_remote_copy(
            src_ref=arrived.at[step, slot],
            dst_ref=arrived.at[step, slot if source is None else source],
            send_sem=sends.at[step],
            recv_sem=recvs.at[step],
            device_id={"ao": target},
            device_id_type=MESH,
        )

    def x_copy(step, source=None):
        return slot_copy(step, me, x_send, x_recv, far, source)

    def c_copy(step, source=None):
        return slot_copy(step, me, c_send, c_recv, near, source)

    def f_copy(step, source=None):
        return slot_copy(step, far, f_send, f_recv, near, source)

    def send_chunk(step):
        for hop in range(1, aux):
            outgoing[hop - 1, step] = form(lax.rem(me_z + hop, aux), step)
            z_copy(step, hop).start()
        arrived[step, me, me_z] = form(me_z, step)

    def behind(hop):
        return lax.rem(me_z + aux - hop, aux)

    pl.semaphore_wait(barrier, aux + 1)
    send_chunk(0)
    for hop in range(1, aux):
        w_copy(hop).start()
    for step in range(1, chunks):
        send_chunk(step)

    total[...] = jnp.zeros_like(total)
    columns = across(eye(8, batch_coef.shape[1], BF16), batch_coef[...])

    def build_weights():
        for hop in range(1, aux):
            w_copy(hop, behind(hop)).wait_recv()
        for part in range(2):
            lanes = slice(part * (functions // 2), (part + 1) * (functions // 2))
            for z in range(aux):
                block = coef[z].astype(F32)[part * occ : (part + 1) * occ]
                for orbit in range(4):
                    first = (orbit * aux + z) * occ
                    coef_t[first : first + occ, :] = block * columns[orbit : orbit + 1, lanes]
            weights[lanes, :] = coef_t[...].T.astype(BF16)

    def compute(step):
        for pair_of in range(2 * aux):
            blocks = [
                arrived[step, source // aux, source % aux].astype(F32)
                for source in (2 * pair_of, 2 * pair_of + 1)
            ]
            for part in range(2):
                packed[2 * occ * pair_of : 2 * occ * (pair_of + 1), part * half : (part + 1) * half] = (
                    jnp.concatenate(
                        [block[part * occ : (part + 1) * occ] for block in blocks], axis=0
                    ).astype(BF16)
                )
        fetch(step).wait()
        slab = slabs.at[step % SLOTS]

        @pl.loop(0, functions // ROWS)
        def _(index):
            rows = pl.ds(pl.multiple_of(index * ROWS, ROWS), ROWS)
            rounded = jnp.dot(
                weights[rows, :], packed[...], preferred_element_type=F32
            ).astype(BF16)
            amp[rows, step * CHUNK : (step + 1) * CHUNK] = rounded
            wide = rounded.astype(F32)
            for axis_dir in range(3):
                product = slab[axis_dir, rows, :].astype(F32) * wide
                lanes = product[:, :128]
                for first in range(128, CHUNK, 128):
                    lanes = lanes + product[:, first : first + 128]
                total[axis_dir, rows, :] += lanes

        if step + SLOTS < chunks:
            fetch(step + SLOTS).start()

    for turn in range(chunks + 2):
        if turn < chunks:
            for hop in range(1, aux):
                z_copy(turn, hop, behind(hop)).wait_recv()
            x_copy(turn).start()
            c_copy(turn).start()
        if turn == 0:
            build_weights()
        if 1 <= turn <= chunks:
            x_copy(turn - 1, far).wait_recv()
            f_copy(turn - 1).start()
        if turn >= 2:
            c_copy(turn - 2, near).wait_recv()
            f_copy(turn - 2, near_far).wait_recv()
            compute(turn - 2)

    atom = lax.broadcasted_iota(jnp.int32, (atoms, functions), 0)
    onehot = (owner[...] == atom).astype(F32)
    sums = jnp.concatenate(
        [
            jnp.dot(onehot, total[axis_dir], precision=lax.Precision.HIGHEST, preferred_element_type=F32)
            for axis_dir in range(3)
        ],
        axis=0,
    )
    grad[...] = across(jnp.ones((8, 128), F32), sums, precision=lax.Precision.HIGHEST)

    for hop in range(1, aux):
        w_copy(hop).wait_send()
    for step in range(chunks):
        for hop in range(1, aux):
            z_copy(step, hop).wait_send()
        x_copy(step).wait_send()
        c_copy(step).wait_send()
        f_copy(step).wait_send()


def leave_kernel(held, out, sems):
    rows = held.shape[0] // LEAVE
    copies = [
        pltpu.make_async_copy(
            held.at[pl.ds(part * rows, rows)], out.at[pl.ds(part * rows, rows)], sems.at[part]
        )
        for part in range(LEAVE)
    ]
    for copy in copies:
        copy.start()
    for copy in copies:
        copy.wait()


def fused(aux, pair_ints, batch_energy, occ_energy, occ_coef, batch_coef, deriv, owner):
    occ = pair_ints.shape[1]
    functions, width = deriv.shape[1], deriv.shape[2]
    chunks = width // CHUNK
    atoms = ATOM_DEV * aux * 4
    depth = 4 * aux * occ
    vmem = pl.BlockSpec(memory_space=pltpu.VMEM)
    dma = pltpu.SemaphoreType.DMA
    amp, grad = pl.pallas_call(
        functools.partial(fused_kernel, aux, atoms),
        out_shape=(
            pltpu.VMEM((functions, width), BF16),
            jax.ShapeDtypeStruct((8, 3 * atoms), F32),
        ),
        in_specs=[
            vmem,
            pl.BlockSpec(memory_space=pltpu.SMEM),
            vmem,
            vmem,
            vmem,
            pl.BlockSpec(memory_space=pl.ANY),
            vmem,
        ],
        out_specs=(vmem, vmem),
        scratch_shapes=[
            pltpu.VMEM((aux - 1, chunks, 2 * occ, CHUNK // 2), BF16),
            pltpu.VMEM((chunks, 4, aux, 2 * occ, CHUNK // 2), BF16),
            pltpu.VMEM((aux, 2 * occ, functions // 2), BF16),
            pltpu.VMEM((depth, functions // 2), F32),
            pltpu.VMEM((functions, depth), BF16),
            pltpu.VMEM((depth, CHUNK), BF16),
            pltpu.VMEM((SLOTS, 3, functions, CHUNK), BF16),
            pltpu.VMEM((3, functions, 128), F32),
            dma((chunks, aux - 1)),
            dma((chunks, aux - 1)),
            dma((aux - 1,)),
            dma((aux - 1,)),
            dma((chunks,)),
            dma((chunks,)),
            dma((chunks,)),
            dma((chunks,)),
            dma((chunks,)),
            dma((chunks,)),
            dma((SLOTS,)),
        ],
        compiler_params=pltpu.CompilerParams(
            collective_id=0, has_side_effects=True, vmem_limit_bytes=42 << 20
        ),
    )(
        pair_ints,
        batch_energy,
        occ_energy.reshape(1, -1),
        occ_coef,
        batch_coef,
        deriv,
        owner.reshape(1, -1),
    )
    amp = pl.pallas_call(
        leave_kernel,
        out_shape=jax.ShapeDtypeStruct((functions, width), BF16),
        in_specs=[vmem],
        out_specs=pl.BlockSpec(memory_space=pl.ANY),
        scratch_shapes=[dma((LEAVE,))],
        compiler_params=pltpu.CompilerParams(vmem_limit_bytes=1 << 20),
    )(amp)
    totals = lax.psum(grad[:1], ("aux", "ao")).reshape(3, atoms)
    own = lax.axis_index(("aux", "ao")) * ATOM_DEV
    return amp, lax.dynamic_slice_in_dim(totals, own, ATOM_DEV, 1)


def staged(pair_ints, batch_energy, occ_energy, occ_coef, batch_coef, deriv, owner):
    scale = 2.0 / (batch_energy[:, None] + occ_energy[None, :])
    formed = (pair_ints.astype(F32) * scale[:, :, None]).astype(BF16)
    arrived = lax.all_to_all(formed, "aux", split_axis=2, concat_axis=1, tiled=True)
    coef_all = lax.all_gather(occ_coef, "aux", axis=1, tiled=True)
    column = batch_coef.astype(F32)
    gathered = lax.all_gather(arrived, "ao", axis=0, tiled=True)
    running = jnp.zeros((coef_all.shape[0], arrived.shape[2]), F32)
    for orbit in range(gathered.shape[0]):
        running = running + column[:, orbit : orbit + 1] * jnp.dot(
            coef_all, gathered[orbit], preferred_element_type=F32
        )
    amp_ao = running.astype(BF16)
    per_func = jnp.einsum("xnp,np->xn", deriv, amp_ao, preferred_element_type=F32)
    atoms = ATOM_DEV * lax.axis_size("aux") * lax.axis_size("ao")
    onehot = (owner[:, None] == jnp.arange(atoms, dtype=jnp.int32)[None, :]).astype(F32)
    partial_grad = jnp.dot(per_func, onehot, precision=lax.Precision.HIGHEST)
    totals = lax.psum(partial_grad, ("aux", "ao"))
    own = lax.axis_index(("aux", "ao")) * ATOM_DEV
    return amp_ao, lax.dynamic_slice_in_dim(totals, own, ATOM_DEV, 1)


def local(*args):
    aux, ao = lax.axis_size("aux"), lax.axis_size("ao")
    occ, width = args[0].shape[1], args[5].shape[2]
    if ao == 4 and aux * ao * occ <= 512 and occ % 8 == 0 and width % CHUNK == 0:
        return fused(aux, *args)
    return staged(*args)


def solution(mesh):
    return jax.shard_map(
        local,
        mesh=mesh,
        in_specs=(
            P(("batch", "ao"), "aux", None),
            P(("batch", "ao")),
            P("aux"),
            P("ao", "aux"),
            P("ao", "batch"),
            P(None, "ao", "aux"),
            P("ao"),
        ),
        out_specs=(P(("batch", "ao"), "aux"), P(None, ("batch", "aux", "ao"))),
        check_vma=False,
    )
```

time: 534 us -> 118 us (0.22)
  matrix products: 164 us -> 0 us
  local copies, waits for them, and re-layouts: 143 us -> 17.5 us
  other arithmetic: 115 us -> 0 us
  Pallas kernels: 0 us -> 66.8 us
  blocking collectives: 77.6 us -> 32 us
  waiting for transfers between devices: 17.6 us -> 0 us
  between operations: 14.8 us -> 1.31 us
    dot_general x6 -> x0, matrix products: 164 us -> none  [the longest x1 87.8 us: local(): jnp.einsum('xnp,np->xn', deriv, amp_ao, preferred_element_type=jnp.float32)]
    unnamed x1 -> x0, other arithmetic: 113 us -> none
    pallas_call x0 -> x2, Pallas kernels: none -> 66.8 us  [the longest x1 61.2 us: fused(): pl.pallas_call(functools.partial(fused_kernel, aux, atoms), out_shape=(pl...]
    add x1 -> x0, local copies, waits for them, and re-layouts: 62.4 us -> none  [local(): running + column * jnp.dot(coef_all, gathered[orbit], preferred_element_t...]
    all_to_all x1 -> x0, blocking collectives: 30.4 us -> none  [local(): lax.all_to_all(formed, 'aux', split_axis=2, concat_axis=1, tiled=True)]
    unnamed x12 -> x6, local copies, waits for them, and re-layouts: 43.9 us -> 14.7 us
    all_to_all x3 -> x0, local copies, waits for them, and re-layouts: 20.3 us -> none  [local(): lax.all_to_all(formed, 'aux', split_axis=2, concat_axis=1, tiled=True)]
    all_gather x1 -> x0, waiting for transfers between devices: 17.6 us -> none  [local(): gathered = lax.all_gather(arrived, 'ao', axis=0, tiled=True)]
  transfers between devices with their start and end apart: 1 -> 0, of which waited for: 1 -> 0; matrix products, arithmetic and copies ran while one was open for 0% -> 0% of each run, Pallas kernels for 0% -> 0%
where the time goes in v1:
time: 118 us
  Pallas kernels  66.8 us (57%)
  blocking collectives  32 us (27%)
  local copies, waits for them, and re-layouts  17.5 us (15%)
  between operations  1.31 us (1%)
    pallas_call x1, Pallas kernels, fused(): pl.pallas_call(functools.partial(fused_kernel, aux, atoms), out_shape=(pl...  61.2 us
    psum x1, blocking collectives, fused(): totals = lax.psum(grad[:1], ('aux', 'ao')).reshape(3, atoms)  32 us
    unnamed x6, local copies, waits for them, and re-layouts  14.7 us
    pallas_call x1, Pallas kernels, fused(): pl.pallas_call(leave_kernel, out_shape=jax.ShapeDtypeStruct((functions, w...  5.64 us

profile of v1, /device:TPU:0, one launch (start us, length us, event | category | flops | bytes accessed | tf_op | source)
XLA Modules:
  0.0 117.6 jit_solution(2324305986201975798)
XLA Ops:
  0.6 1.7 %copy.10.batch_coef = bf16[1536,4]{1,0:T(8,128)(2,1)} copy(bf16[1536,4]{0,1:T(4,128)(2,1)} %param.11) | data formatting | bytes 24576 | tf_op args[4]
  2.3 1.8 %copy.9.occ_coef = bf16[1536,24]{1,0:T(8,128)(2,1)} copy(bf16[1536,24]{0,1:T(8,128)(2,1)} %param.10) | data formatting | bytes 147456 | tf_op args[3]
  4.1 1.3 %reshape.14.owner = s32[1,1536]{1,0:T(1,128)} reshape(s32[1536]{0:T(1024)} %param.13) | data formatting | bytes 12288 | tf_op jit(solution)/shard_map/reshape | solution.py:288
  6.0 61.2 %shard_map.86 = (bf16[1536,5120]{1,0:T(8,128)(2,1)S(1)}, f32[8,144]{1,0:T(8,128)}) custom-call(bf16[1,24,20480]{2,1,0:T(8,128)(2,1)} %pair.1, f32[1]{0:T(128)S(6)} %copy.11.batch_energy, f32[1,24]{1,0:T(1,128)} %bitcast.1, bf16[1536,24]{1,0:T(8,128)(2,1)} %copy.9.occ_coef, bf16[1536,4]{1,0:T(8,128)(2,1)} %copy.10.batch_coef, bf16[3,1536,5120]{2,1,0:T(8,128)(2,1)} %deriv.1, ...), custom_call_target="tpu_custom_call" | custom-call | tf_op jit(solution)/shard_map/pallas_call | solution.py:241
  67.2 0.0 copy-start
  67.2 5.8 %copy-done = bf16[1536,5120]{1,0:T(8,128)(2,1)} copy-done((bf16[1536,5120]{1,0:T(8,128)(2,1)}, bf16[1536,5120]{1,0:T(8,128)(2,1)S(1)}, u32[]{:S(2)}) %copy-start) | copy-done | bytes 15728664
  73.1 0.7 slice_reduce_fusion
  73.8 0.1 reshape.15
  73.9 32.0 %psum.7 = f32[3,48]{1,0:T(4,128)S(1)} all-reduce(f32[3,48]{1,0:T(4,128)S(1)} %reshape.15), channel_id=1, replica_groups=mesh['batch'=2,'aux'=4,'ao'=4] {'aux','ao'}, use_global_device_ids=true, to_apply=%region_0.0 | all-reduce | flops 144 | bytes 1152 | tf_op jit(solution)/shard_map/psum | solution.py:298
  105.9 0.7 constant_dynamic-slice_fusion
  106.5 0.0 copy-start.1
  106.5 5.5 %copy-done.1 = bf16[1536,5120]{1,0:T(8,128)(2,1)S(1)} copy-done((bf16[1536,5120]{1,0:T(8,128)(2,1)S(1)}, bf16[1536,5120]{1,0:T(8,128)(2,1)}, u32[]{:S(2)}) %copy-start.1) | copy-done | bytes 15728664
  112.0 5.6 %shard_map.87 = bf16[1536,5120]{1,0:T(8,128)(2,1)} custom-call(bf16[1536,5120]{1,0:T(8,128)(2,1)S(1)} %copy-done.1), custom_call_target="tpu_custom_call" | custom-call | tf_op jit(solution)/shard_map/pallas_call | solution.py:290
Async XLA Ops:
  67.2 5.8 %copy-start = (bf16[1536,5120]{1,0:T(8,128)(2,1)}, bf16[1536,5120]{1,0:T(8,128)(2,1)S(1)}, u32[]{:S(2)}) copy-start(bf16[1536,5120]{1,0:T(8,128)(2,1)S(1)} %get-tuple-element.4.held) | copy-start | bytes 47185924
  106.5 5.5 %copy-start.1 = (bf16[1536,5120]{1,0:T(8,128)(2,1)S(1)}, bf16[1536,5120]{1,0:T(8,128)(2,1)}, u32[]{:S(2)}) copy-start(bf16[1536,5120]{1,0:T(8,128)(2,1)} %copy-done) | copy-start | bytes 47185924

commit v2 on v1

--- a/solution.py
+++ b/solution.py
@@ -32,14 +32,14 @@
 def fused_kernel(
     aux, atoms, pair, batch_energy, occ_energy, occ_coef, batch_coef, deriv, owner,
     amp, grad,
-    outgoing, arrived, coef, coef_t, weights, packed, slabs, total,
-    z_send, z_recv, w_send, w_recv, x_send, x_recv, c_send, c_recv, f_send, f_recv, d_sem,
+    shares, outgoing, arrived, coef, coef_t, weights, packed, slabs, total,
+    z_send, z_recv, w_send, w_recv, x_send, x_recv, c_send, c_recv, f_send, f_recv, s_send, s_recv, d_sem,
 ):
     occ = pair.shape[1]
     width = pair.shape[2] // aux
     chunks = width // CHUNK
     half = CHUNK // 2
-    functions = occ_coef.shape[0]
+    functions = occ_coef.shape[1]
     me_z, me = lax.axis_index("aux"), lax.axis_index("ao")
     far = lax.rem(me + 2, 4)
     near = me + 1 - 2 * lax.rem(me, 2)
@@ -58,10 +58,10 @@
         pl.semaphore_signal(
             barrier, inc=1, device_id={"aux": lax.rem(me_z + hop, aux)}, device_id_type=MESH
         )
-    for other in (far, near):
+    for other in (far, near, near_far):
         pl.semaphore_signal(barrier, inc=1, device_id={"ao": other}, device_id_type=MESH)
 
-    turned = across(eye(occ, occ, BF16), occ_coef[...])
+    turned = occ_coef[...].astype(F32)
     coef[me_z] = jnp.concatenate(
         [turned[:, : functions // 2], turned[:, functions // 2 :]], axis=0
     ).astype(BF16)
@@ -124,7 +124,7 @@
     def behind(hop):
         return lax.rem(me_z + aux - hop, aux)
 
-    pl.semaphore_wait(barrier, aux + 1)
+    pl.semaphore_wait(barrier, aux + 2)
     send_chunk(0)
     for hop in range(1, aux):
         w_copy(hop).start()
@@ -132,7 +132,7 @@
         send_chunk(step)
 
     total[...] = jnp.zeros_like(total)
-    columns = across(eye(8, batch_coef.shape[1], BF16), batch_coef[...])
+    columns = batch_coef[...].astype(F32)
 
     def build_weights():
         for hop in range(1, aux):
@@ -196,7 +196,7 @@
             compute(turn - 2)
 
     atom = lax.broadcasted_iota(jnp.int32, (atoms, functions), 0)
-    onehot = (owner[...] == atom).astype(F32)
+    onehot = (owner[...][None, :] == atom).astype(F32)
     sums = jnp.concatenate(
         [
             jnp.dot(onehot, total[axis_dir], precision=lax.Precision.HIGHEST, preferred_element_type=F32)
@@ -204,7 +204,29 @@
         ],
         axis=0,
     )
-    grad[...] = across(jnp.ones((8, 128), F32), sums, precision=lax.Precision.HIGHEST)
+    shares[0, me_z] = across(jnp.ones((8, 128), F32), sums, precision=lax.Precision.HIGHEST)
+
+    def s_copy(level, hop, mine, count, name, source=None):
+        return pltpu.make_async_remote_copy(
+            src_ref=shares.at[level, mine],
+            dst_ref=shares.at[level, mine if source is None else source],
+            send_sem=s_send.at[level, hop - 1],
+            recv_sem=s_recv.at[level, hop - 1],
+            device_id={name: lax.rem(mine + hop, count)},
+            device_id_type=MESH,
+        )
+
+    for level, (mine, count, name) in enumerate(((me_z, aux, "aux"), (me, 4, "ao"))):
+        if level == 1:
+            shares[1, me] = functools.reduce(lambda a, b: a + b, [shares[0, z] for z in range(aux)])
+        for hop in range(1, count):
+            s_copy(level, hop, mine, count, name).start()
+        for hop in range(1, count):
+            s_copy(level, hop, mine, count, name, lax.rem(mine + count - hop, count)).wait_recv()
+    grad[...] = functools.reduce(lambda a, b: a + b, [shares[1, ao] for ao in range(4)])
+    for level, (mine, count, name) in enumerate(((me_z, aux, "aux"), (me, 4, "ao"))):
+        for hop in range(1, count):
+            s_copy(level, hop, mine, count, name).wait_send()
 
     for hop in range(1, aux):
         w_copy(hop).wait_send()
@@ -216,7 +238,7 @@
         f_copy(step).wait_send()
 
 
-def leave_kernel(held, out, sems):
+def leave_kernel(held, sums, out, sums_out, sems):
     rows = held.shape[0] // LEAVE
     copies = [
         pltpu.make_async_copy(
@@ -226,6 +248,7 @@
     ]
     for copy in copies:
         copy.start()
+    sums_out[...] = sums[...]
     for copy in copies:
         copy.wait()
 
@@ -255,6 +278,7 @@
         ],
         out_specs=(vmem, vmem),
         scratch_shapes=[
+            pltpu.VMEM((2, max(aux, 4), 8, 3 * atoms), F32),
             pltpu.VMEM((aux - 1, chunks, 2 * occ, CHUNK // 2), BF16),
             pltpu.VMEM((chunks, 4, aux, 2 * occ, CHUNK // 2), BF16),
             pltpu.VMEM((aux, 2 * occ, functions // 2), BF16),
@@ -273,6 +297,8 @@
             dma((chunks,)),
             dma((chunks,)),
             dma((chunks,)),
+            dma((2, max(aux, 4) - 1)),
+            dma((2, max(aux, 4) - 1)),
             dma((SLOTS,)),
         ],
         compiler_params=pltpu.CompilerParams(
@@ -282,20 +308,23 @@
         pair_ints,
         batch_energy,
         occ_energy.reshape(1, -1),
-        occ_coef,
-        batch_coef,
+        occ_coef.T,
+        batch_coef.T,
         deriv,
-        owner.reshape(1, -1),
+        owner,
     )
-    amp = pl.pallas_call(
+    amp, grad = pl.pallas_call(
         leave_kernel,
-        out_shape=jax.ShapeDtypeStruct((functions, width), BF16),
-        in_specs=[vmem],
-        out_specs=pl.BlockSpec(memory_space=pl.ANY),
+        out_shape=(
+            jax.ShapeDtypeStruct((functions, width), BF16),
+            jax.ShapeDtypeStruct(grad.shape, F32),
+        ),
+        in_specs=[vmem, vmem],
+        out_specs=(pl.BlockSpec(memory_space=pl.ANY), vmem),
         scratch_shapes=[dma((LEAVE,))],
         compiler_params=pltpu.CompilerParams(vmem_limit_bytes=1 << 20),
-    )(amp)
-    totals = lax.psum(grad[:1], ("aux", "ao")).reshape(3, atoms)
+    )(amp, grad)
+    totals = grad[0].reshape(3, atoms)
     own = lax.axis_index(("aux", "ao")) * ATOM_DEV
     return amp, lax.dynamic_slice_in_dim(totals, own, ATOM_DEV, 1)
 

time: 118 us -> 77.6 us (0.66)
  blocking collectives: 32 us -> 0 us
  local copies, waits for them, and re-layouts: 17.5 us -> 1.45 us
  Pallas kernels: 66.8 us -> 74.6 us
    psum x1 -> x0, blocking collectives: 32 us -> none  [fused(): totals = lax.psum(grad[:1], ('aux', 'ao')).reshape(3, atoms)]
    unnamed x6 -> x2, local copies, waits for them, and re-layouts: 14.7 us -> 0.69 us
    pallas_call x1, Pallas kernels: 61.2 us -> 69 us  [fused(): pl.pallas_call(functools.partial(fused_kernel, aux, atoms), out_shape=(pl...]
    reshape x2 -> x0, local copies, waits for them, and re-layouts: 1.37 us -> none  [the longest x1 1.29 us: fused(): owner.reshape(1, -1)]
where the time goes in v2:
time: 77.6 us; the launch traced here: 77.4 us
  Pallas kernels  74.6 us (96%)
  local copies, waits for them, and re-layouts  1.45 us (2%)
  between operations  1.3 us (2%)
    pallas_call x1, Pallas kernels, fused(): pl.pallas_call(functools.partial(fused_kernel, aux, atoms), out_shape=(pl...  69 us
    pallas_call x1, Pallas kernels, fused(): pl.pallas_call(leave_kernel, out_shape=(jax.ShapeDtypeStruct((functions,...  5.65 us

profile of v2, /device:TPU:0, one launch (start us, length us, event | category | flops | bytes accessed | tf_op | source)
XLA Modules:
  0.0 77.4 jit_solution(15453073431316637559)
XLA Ops:
  1.3 69.0 %shard_map.86 = (bf16[1536,5120]{1,0:T(8,128)(2,1)S(1)}, f32[8,144]{1,0:T(8,128)}) custom-call(bf16[1,24,20480]{2,1,0:T(8,128)(2,1)} %pair.1, f32[1]{0:T(128)S(6)} %copy.9.batch_energy, f32[1,24]{1,0:T(1,128)} %bitcast.5, bf16[24,1536]{1,0:T(8,128)(2,1)} %bitcast.3, bf16[4,1536]{1,0:T(4,128)(2,1)} %bitcast.4, bf16[3,1536,5120]{2,1,0:T(8,128)(2,1)} %deriv.1, ...), custom_call_target="tpu_custom_call" | custom-call | tf_op jit(solution)/shard_map/pallas_call | solution.py:264
  70.3 0.0 copy-start
  70.3 0.7 copy-done
  71.0 5.6 %shard_map.87 = (bf16[1536,5120]{1,0:T(8,128)(2,1)}, f32[8,144]{1,0:T(8,128)S(1)}) custom-call(bf16[1536,5120]{1,0:T(8,128)(2,1)S(1)} %get-tuple-element.6.held, f32[8,144]{1,0:T(8,128)S(1)} %copy-done), custom_call_target="tpu_custom_call" | custom-call | tf_op jit(solution)/shard_map/pallas_call | solution.py:316
  76.6 0.1 reshape_squeeze.3
  76.7 0.7 constant_dynamic-slice_fusion
  (1 shorter events, 0.0 us)
Async XLA Ops:
  70.3 0.7 copy-start
